TPU v7x, 512 devices: a whole 4x8x8 slice. The times are simulated.
512 devices in a mesh: sea: 32 (over y, x_lo, core), fault: 16 (over z, x_hi).
Axes of the slice: x: 4 (x_hi: 2, x_lo: 2; x = x_hi * 2 + x_lo), y: 8, z: 8, core: 2. Of those that a mesh axis runs over, the one named last changes fastest.
Arguments:
- slip_rate: bfloat16 [65536, 128], P(('fault', 'sea')), may hold values from -6 to 6
- near_blocks: bfloat16 [32, 16, 8, 256, 256], P('sea', 'fault'), may hold values from -0.375 to 0.375
- near_rows: int32 [32, 16, 8], P('sea', 'fault'), may hold values from 0 to 15
- near_cols: int32 [32, 16, 8], P('sea', 'fault'), may hold values from 0 to 15
- near_scale: float32 [32, 16, 8], P('sea', 'fault'), may hold values from 0.1 to 0.5
- far_left: bfloat16 [32, 16, 24, 48, 256], P('sea', 'fault'), may hold values from -0.875 to 0.875
- far_right: bfloat16 [32, 16, 24, 48, 256], P('sea', 'fault'), may hold values from -0.375 to 0.375
- far_rows: int32 [32, 16, 24], P('sea', 'fault'), may hold values from 0 to 15
- far_cols: int32 [32, 16, 24], P('sea', 'fault'), may hold values from 0 to 15
- far_rank: int32 [32, 16, 24], P('sea', 'fault'), may hold values from 16 to 48, as said below
- far_scale: float32 [32, 16, 24], P('sea', 'fault'), may hold values from 0.1 to 0.5
- sea_depth: float32 [512, 256], P('sea', 'fault'), may hold values from 0.3 to 1
- wet_mask: int32 [512, 256], P('sea', 'fault'), may hold values 0 or 1
Outputs:
- uplift: float32 [512, 256, 128], P('sea', 'fault')
- sea_level: float32 [512, 256, 128], P('sea', 'fault')
Inputs may be any that keep to these rules, and one draw needn't show every extreme that they name: `far_rank`: block 0 of every device has rank 48; every rank is at least 16.
All inputs are finite; a program needn't handle non-finite values. No bound on the sum of `wet_mask` on one device may be relied on, other than what follows from the above.
Results may differ from a plain program's by a relative error of at most 0.0024.
Values may be sent and summed in bfloat16 or wider, within the bound.
A program may use at most 64 MiB of HBM per device.

v0:
```python
import jax
import jax.numpy as jnp
from jax import lax
from jax.sharding import PartitionSpec as P

STEPS = 6
gravity_step = 0.7
height_step = 0.7


def extended(cells, sides, width):
    for axis, dim in sides:
        count = lax.axis_size(axis)
        ends = count - 1
        head = lax.slice_in_dim(cells, 0, width, axis=dim)
        tail = lax.slice_in_dim(cells, cells.shape[dim] - width, cells.shape[dim], axis=dim)
        cells = jnp.concatenate(
            [
                lax.ppermute(tail, axis, [(i, (i + 1) % count) for i in range(ends)]),
                cells,
                lax.ppermute(head, axis, [((i + 1) % count, i) for i in range(ends)]),
            ],
            axis=dim,
        )
    return cells


def advance(height, east_flow, north_flow, depth_pad):
    new_east = east_flow[1:-1, :-1] - gravity_step * (height[1:-1, 1:] - height[1:-1, :-1])
    east_depth = jnp.minimum(depth_pad[1:-1, :-1], depth_pad[1:-1, 1:])
    flux_east = east_depth[:, :, None] * new_east
    new_north = north_flow[:-1, 1:-1] - gravity_step * (height[1:, 1:-1] - height[:-1, 1:-1])
    north_depth = jnp.minimum(depth_pad[:-1, 1:-1], depth_pad[1:, 1:-1])
    flux_north = north_depth[:, :, None] * new_north
    change = flux_east[:, 1:] - flux_east[:, :-1] + flux_north[1:] - flux_north[:-1]
    new_height = height[1:-1, 1:-1] - height_step * change
    return (new_height, new_east[:, 1:], new_north[1:])


def on_device(
    slip_rate,
    near_blocks,
    near_rows,
    near_cols,
    near_scale,
    far_left,
    far_right,
    far_rows,
    far_cols,
    far_rank,
    far_scale,
    sea_depth,
    wet_mask,
):
    brick_y, brick_x = sea_depth.shape
    fault_count = lax.axis_size("fault")
    leaf_size = near_blocks.shape[-1]
    rank_pad = far_left.shape[-2]
    members = slip_rate.shape[1]
    leaf_count = brick_y * brick_x * fault_count // leaf_size
    targets = jnp.arange(leaf_count)
    gathered = lax.all_gather(slip_rate, "sea", axis=0, tiled=True)
    leaves = gathered.reshape(-1, leaf_size, members)
    near_slip = leaves[near_cols[0, 0]]
    near_term = jnp.einsum(
        "bij,bjs->bis", near_blocks[0, 0], near_slip, preferred_element_type=jnp.float32
    )
    near_weight = (near_rows[0, 0][:, None] == targets).astype(jnp.float32) * near_scale[0, 0][
        :, None
    ]
    total = jnp.einsum("br,bis->ris", near_weight, near_term, precision=lax.Precision.HIGHEST)
    far_slip = leaves[far_cols[0, 0]]
    coeffs = jnp.einsum(
        "bkc,bcs->bks", far_right[0, 0], far_slip, preferred_element_type=jnp.float32
    )
    kept = jnp.arange(rank_pad)[None, :, None] < far_rank[0, 0][:, None, None]
    coeffs = jnp.where(kept, coeffs, jnp.float32(0.0)).astype(jnp.bfloat16)
    far_term = jnp.einsum(
        "bki,bks->bis", far_left[0, 0], coeffs, preferred_element_type=jnp.float32
    )
    far_weight = (far_rows[0, 0][:, None] == targets).astype(jnp.float32) * far_scale[0, 0][:, None]
    total = total + jnp.einsum("br,bis->ris", far_weight, far_term, precision=lax.Precision.HIGHEST)
    partial_value = total.reshape(brick_y, fault_count, brick_x, members)
    ordered = jnp.transpose(partial_value, (1, 0, 2, 3))
    summed = lax.psum_scatter(ordered, "fault", scatter_dimension=0, tiled=True)
    uplift = summed[0]
    wet = wet_mask.astype(jnp.float32)
    depth_cell = sea_depth * wet
    height = uplift * wet[:, :, None]
    east_flow = jnp.zeros_like(height)
    north_flow = jnp.zeros_like(height)
    depth_pad = extended(depth_cell, (("sea", 0), ("fault", 1)), 1)
    for step_index in range(STEPS):
        padded = (
            extended(height, (("sea", 0), ("fault", 1)), 1),
            extended(east_flow, (("sea", 0), ("fault", 1)), 1),
            extended(north_flow, (("sea", 0), ("fault", 1)), 1),
        )
        height, east_flow, north_flow = advance(padded[0], padded[1], padded[2], depth_pad)
    return (uplift, height)


def solution(mesh):
    placed = (
        P(("fault", "sea"), None),
        P("sea", "fault", None, None, None),
        P("sea", "fault", None),
        P("sea", "fault", None),
        P("sea", "fault", None),
        P("sea", "fault", None, None, None),
        P("sea", "fault", None, None, None),
        P("sea", "fault", None),
        P("sea", "fault", None),
        P("sea", "fault", None),
        P("sea", "fault", None),
        P("sea", "fault"),
        P("sea", "fault"),
    )
    return jax.shard_map(
        on_device,
        mesh=mesh,
        in_specs=placed,
        out_specs=(P("sea", "fault", None), P("sea", "fault", None)),
        check_vma=False,
    )
```

profile of v0, /device:TPU:288, one launch (start us, length us, event | category | flops | bytes accessed | tf_op | source)
XLA Modules:
  0.0 510.8 jit_solution(5362446358330737596)
XLA Ops:
  10.0 66.4 %all-gather.2.cloned.1.call-done = bf16[4096,128]{1,0:T(8,128)(2,1)} async-done(((bf16[128,128]{1,0:T(8,128)(2,1)}), bf16[4096,128]{1,0:T(8,128)(2,1)}) %all-gather.2.cloned.1.call-update) | async-done | bytes 1048592 | tf_op jit(solution)/shard_map/all_gather | solution.py:62
  76.4 2.1 gather_fusion.1
  78.5 3.8 fusion.5
  82.3 3.6 copy.17
  91.3 2.0 fusion.2
  93.3 2.0 copy.19
  95.3 2.1 collective-permute-start.4
  97.4 5.5 %collective-permute-start.5 = (f32[1,16,128]{2,1,0:T(8,128)S(1)}, f32[1,16,128]{2,1,0:T(8,128)S(1)}, u32[]{:S(2)}, u32[]{:S(2)}) collective-permute-start(f32[1,16,128]{2,1,0:T(8,128)S(1)} %broadcast.92), channel_id=1, source_target_pairs={{16,0},{32,16},{48,32},{64,48},{80,64},{96,80},{112,96},{128,112},... | collective-permute-start | bytes 24584 | tf_op jit(solution)/shard_map/ppermute | solution.py:21
  103.0 1.9 collective-permute-start
  105.0 5.8 %collective-permute-start.1 = (f32[1,16]{1,0:T(1,128)S(1)}, f32[1,16]{1,0:T(1,128)S(1)}, u32[]{:S(2)}, u32[]{:S(2)}) collective-permute-start(f32[1,16]{1,0:T(1,128)S(1)} %get-tuple-element.58), channel_id=1, source_target_pairs={{16,0},{32,16},{48,32},{64,48},{80,64},{96,80},{112,96},{128,112},... | collective-permute-start | bytes 200 | tf_op jit(solution)/shard_map/ppermute | solution.py:21
  112.1 4.9 collective-permute-start.2
  117.0 4.6 collective-permute-start.3
  121.6 2.5 collective-permute-done.3
  124.1 184.5 %reduce-scatter.2.cloned.1.call-done = f32[1,16,16,128]{3,2,1,0:T(8,128)} async-done(((f32[16,16,16,128]{3,2,1,0:T(8,128)}), f32[1,16,16,128]{3,2,1,0:T(8,128)}) %reduce-scatter.2.cloned.1.call-update) | async-done | bytes 131088 | tf_op jit(solution)/shard_map/reduce_scatter | solution.py:85
  309.7 1.9 collective-permute-start.7
  311.6 5.8 %collective-permute-start.8 = (f32[1,16,128]{2,1,0:T(8,128)S(1)}, f32[1,16,128]{2,1,0:T(8,128)S(1)}, u32[]{:S(2)}, u32[]{:S(2)}) collective-permute-start(f32[1,16,128]{2,1,0:T(8,128)S(1)} %get-tuple-element.54), channel_id=1, source_target_pairs={{16,0},{32,16},{48,32},{64,48},{80,64},{96,80},{112,96},{128,112},... | collective-permute-start | bytes 24584 | tf_op jit(solution)/shard_map/ppermute | solution.py:21
  317.4 2.5 collective-permute-start.6
  319.9 3.9 collective-permute-start.10
  323.8 5.6 %collective-permute-start.9 = (f32[18,1,128]{2,1,0:T(1,128)S(1)}, f32[18,1,128]{2,1,0:T(1,128)S(1)}, u32[]{:S(2)}, u32[]{:S(2)}) collective-permute-start(f32[18,1,128]{2,1,0:T(1,128)S(1)} %get-tuple-element.42), channel_id=1, source_target_pairs={{1,0},{2,1},{3,2},{4,3},{5,4},{6,5},{7,6},{8,7},{9,8},{10,9},{11,1... | collective-permute-start | bytes 27656 | tf_op jit(solution)/shard_map/ppermute | solution.py:21
  329.5 1.9 collective-permute-start.18
  331.6 1.9 collective-permute-start.11
  333.6 5.8 %collective-permute-start.12 = (f32[1,16,128]{2,1,0:T(8,128)S(1)}, f32[1,16,128]{2,1,0:T(8,128)S(1)}, u32[]{:S(2)}, u32[]{:S(2)}) collective-permute-start(f32[1,16,128]{2,1,0:T(8,128)S(1)} %get-tuple-element.31), channel_id=1, source_target_pairs={{16,0},{32,16},{48,32},{64,48},{80,64},{96,80},{112,96},{128,112},... | collective-permute-start | bytes 24584 | tf_op jit(solution)/shard_map/ppermute | solution.py:21
  339.5 1.9 collective-permute-start.14
  341.4 5.8 %collective-permute-start.15 = (f32[1,16,128]{2,1,0:T(8,128)S(1)}, f32[1,16,128]{2,1,0:T(8,128)S(1)}, u32[]{:S(2)}, u32[]{:S(2)}) collective-permute-start(f32[1,16,128]{2,1,0:T(8,128)S(1)} %get-tuple-element.52), channel_id=1, source_target_pairs={{16,0},{32,16},{48,32},{64,48},{80,64},{96,80},{112,96},{128,112},... | collective-permute-start | bytes 24584 | tf_op jit(solution)/shard_map/ppermute | solution.py:21
  347.2 4.5 collective-permute-start.13
  351.8 4.9 collective-permute-start.16
  356.7 2.4 collective-permute-start.17
  361.3 4.6 collective-permute-done.17
  366.0 1.9 collective-permute-start.19
  368.0 5.8 %collective-permute-start.20 = (f32[1,16,128]{2,1,0:T(8,128)S(1)}, f32[1,16,128]{2,1,0:T(8,128)S(1)}, u32[]{:S(2)}, u32[]{:S(2)}) collective-permute-start(f32[1,16,128]{2,1,0:T(8,128)S(1)} %get-tuple-element.29), channel_id=1, source_target_pairs={{16,0},{32,16},{48,32},{64,48},{80,64},{96,80},{112,96},{128,112},... | collective-permute-start | bytes 24584 | tf_op jit(solution)/shard_map/ppermute | solution.py:21
  375.7 5.8 %collective-permute-start.23 = (f32[1,16,128]{2,1,0:T(8,128)S(1)}, f32[1,16,128]{2,1,0:T(8,128)S(1)}, u32[]{:S(2)}, u32[]{:S(2)}) collective-permute-start(f32[1,16,128]{2,1,0:T(8,128)S(1)} %get-tuple-element.50), channel_id=1, source_target_pairs={{16,0},{32,16},{48,32},{64,48},{80,64},{96,80},{112,96},{128,112},... | collective-permute-start | bytes 24584 | tf_op jit(solution)/shard_map/ppermute | solution.py:21
  383.5 7.5 %collective-permute-start.24 = (f32[18,1,128]{2,1,0:T(1,128)S(1)}, f32[18,1,128]{2,1,0:T(1,128)S(1)}, u32[]{:S(2)}, u32[]{:S(2)}) collective-permute-start(f32[18,1,128]{2,1,0:T(1,128)S(1)} %get-tuple-element.38), channel_id=1, source_target_pairs={{1,0},{2,1},{3,2},{4,3},{5,4},{6,5},{7,6},{8,7},{9,8},{10,9},{11,1... | collective-permute-start | bytes 27656 | tf_op jit(solution)/shard_map/ppermute | solution.py:21
  395.1 5.1 %collective-permute-done.25 = f32[18,1,128]{2,1,0:T(1,128)S(1)} collective-permute-done((f32[18,1,128]{2,1,0:T(1,128)S(1)}, f32[18,1,128]{2,1,0:T(1,128)S(1)}, u32[]{:S(2)}, u32[]{:S(2)}) %collective-permute-start.25) | collective-permute-done | bytes 9248 | tf_op jit(solution)/shard_map/ppermute | solution.py:19
  400.4 1.9 collective-permute-start.27
  402.3 5.8 %collective-permute-start.28 = (f32[1,16,128]{2,1,0:T(8,128)S(1)}, f32[1,16,128]{2,1,0:T(8,128)S(1)}, u32[]{:S(2)}, u32[]{:S(2)}) collective-permute-start(f32[1,16,128]{2,1,0:T(8,128)S(1)} %get-tuple-element.27), channel_id=1, source_target_pairs={{16,0},{32,16},{48,32},{64,48},{80,64},{96,80},{112,96},{128,112},... | collective-permute-start | bytes 24584 | tf_op jit(solution)/shard_map/ppermute | solution.py:21
  410.1 5.8 %collective-permute-start.31 = (f32[1,16,128]{2,1,0:T(8,128)S(1)}, f32[1,16,128]{2,1,0:T(8,128)S(1)}, u32[]{:S(2)}, u32[]{:S(2)}) collective-permute-start(f32[1,16,128]{2,1,0:T(8,128)S(1)} %get-tuple-element.48), channel_id=1, source_target_pairs={{16,0},{32,16},{48,32},{64,48},{80,64},{96,80},{112,96},{128,112},... | collective-permute-start | bytes 24584 | tf_op jit(solution)/shard_map/ppermute | solution.py:21
  417.8 7.5 %collective-permute-start.32 = (f32[18,1,128]{2,1,0:T(1,128)S(1)}, f32[18,1,128]{2,1,0:T(1,128)S(1)}, u32[]{:S(2)}, u32[]{:S(2)}) collective-permute-start(f32[18,1,128]{2,1,0:T(1,128)S(1)} %get-tuple-element.36), channel_id=1, source_target_pairs={{1,0},{2,1},{3,2},{4,3},{5,4},{6,5},{7,6},{8,7},{9,8},{10,9},{11,1... | collective-permute-start | bytes 27656 | tf_op jit(solution)/shard_map/ppermute | solution.py:21
  429.4 5.1 %collective-permute-done.33 = f32[18,1,128]{2,1,0:T(1,128)S(1)} collective-permute-done((f32[18,1,128]{2,1,0:T(1,128)S(1)}, f32[18,1,128]{2,1,0:T(1,128)S(1)}, u32[]{:S(2)}, u32[]{:S(2)}) %collective-permute-start.33) | collective-permute-done | bytes 9248 | tf_op jit(solution)/shard_map/ppermute | solution.py:19
  434.7 1.9 collective-permute-start.35
  436.6 5.8 %collective-permute-start.36 = (f32[1,16,128]{2,1,0:T(8,128)S(1)}, f32[1,16,128]{2,1,0:T(8,128)S(1)}, u32[]{:S(2)}, u32[]{:S(2)}) collective-permute-start(f32[1,16,128]{2,1,0:T(8,128)S(1)} %get-tuple-element.25), channel_id=1, source_target_pairs={{16,0},{32,16},{48,32},{64,48},{80,64},{96,80},{112,96},{128,112},... | collective-permute-start | bytes 24584 | tf_op jit(solution)/shard_map/ppermute | solution.py:21
  444.4 5.8 %collective-permute-start.39 = (f32[1,16,128]{2,1,0:T(8,128)S(1)}, f32[1,16,128]{2,1,0:T(8,128)S(1)}, u32[]{:S(2)}, u32[]{:S(2)}) collective-permute-start(f32[1,16,128]{2,1,0:T(8,128)S(1)} %get-tuple-element.46), channel_id=1, source_target_pairs={{16,0},{32,16},{48,32},{64,48},{80,64},{96,80},{112,96},{128,112},... | collective-permute-start | bytes 24584 | tf_op jit(solution)/shard_map/ppermute | solution.py:21
  452.2 7.5 %collective-permute-start.40 = (f32[18,1,128]{2,1,0:T(1,128)S(1)}, f32[18,1,128]{2,1,0:T(1,128)S(1)}, u32[]{:S(2)}, u32[]{:S(2)}) collective-permute-start(f32[18,1,128]{2,1,0:T(1,128)S(1)} %get-tuple-element.34), channel_id=1, source_target_pairs={{1,0},{2,1},{3,2},{4,3},{5,4},{6,5},{7,6},{8,7},{9,8},{10,9},{11,1... | collective-permute-start | bytes 27656 | tf_op jit(solution)/shard_map/ppermute | solution.py:21
  463.7 5.1 %collective-permute-done.41 = f32[18,1,128]{2,1,0:T(1,128)S(1)} collective-permute-done((f32[18,1,128]{2,1,0:T(1,128)S(1)}, f32[18,1,128]{2,1,0:T(1,128)S(1)}, u32[]{:S(2)}, u32[]{:S(2)}) %collective-permute-start.41) | collective-permute-done | bytes 9248 | tf_op jit(solution)/shard_map/ppermute | solution.py:19
  469.0 1.9 collective-permute-start.43
  470.9 5.8 %collective-permute-start.44 = (f32[1,16,128]{2,1,0:T(8,128)S(1)}, f32[1,16,128]{2,1,0:T(8,128)S(1)}, u32[]{:S(2)}, u32[]{:S(2)}) collective-permute-start(f32[1,16,128]{2,1,0:T(8,128)S(1)} %get-tuple-element.23), channel_id=1, source_target_pairs={{16,0},{32,16},{48,32},{64,48},{80,64},{96,80},{112,96},{128,112},... | collective-permute-start | bytes 24584 | tf_op jit(solution)/shard_map/ppermute | solution.py:21
  478.7 5.8 %collective-permute-start.47 = (f32[1,16,128]{2,1,0:T(8,128)S(1)}, f32[1,16,128]{2,1,0:T(8,128)S(1)}, u32[]{:S(2)}, u32[]{:S(2)}) collective-permute-start(f32[1,16,128]{2,1,0:T(8,128)S(1)} %get-tuple-element.45), channel_id=1, source_target_pairs={{16,0},{32,16},{48,32},{64,48},{80,64},{96,80},{112,96},{128,112},... | collective-permute-start | bytes 24584 | tf_op jit(solution)/shard_map/ppermute | solution.py:21
  486.5 7.5 %collective-permute-start.48 = (f32[18,1,128]{2,1,0:T(1,128)S(1)}, f32[18,1,128]{2,1,0:T(1,128)S(1)}, u32[]{:S(2)}, u32[]{:S(2)}) collective-permute-start(f32[18,1,128]{2,1,0:T(1,128)S(1)} %get-tuple-element.32), channel_id=1, source_target_pairs={{1,0},{2,1},{3,2},{4,3},{5,4},{6,5},{7,6},{8,7},{9,8},{10,9},{11,1... | collective-permute-start | bytes 27656 | tf_op jit(solution)/shard_map/ppermute | solution.py:21
  496.1 7.1 %collective-permute-done.49 = f32[18,1,128]{2,1,0:T(1,128)S(1)} collective-permute-done((f32[18,1,128]{2,1,0:T(1,128)S(1)}, f32[18,1,128]{2,1,0:T(1,128)S(1)}, u32[]{:S(2)}, u32[]{:S(2)}) %collective-permute-start.49) | collective-permute-done | bytes 9248 | tf_op jit(solution)/shard_map/ppermute | solution.py:19
  (162 shorter events, 44.3 us)
Async XLA Ops:
  7.2 69.2 %all-gather.2.cloned.1.call-start = ((), (), s32[]{:S(2)}) async-start(), calls=%async_computation.1 | async-start | bytes 1081344 | tf_op jit(solution)/shard_map/all_gather | solution.py:62
  7.9 300.7 %reduce-scatter.2.cloned.1.call-start = ((), (), s32[]{:S(2)}) async-start(), calls=%async_computation.2 | async-start | bytes 2228224 | tf_op jit(solution)/shard_map/reduce_scatter | solution.py:85
  95.3 222.1 %collective-permute-start.4 = (f32[1,16,128]{2,1,0:T(8,128)S(1)}, f32[1,16,128]{2,1,0:T(8,128)S(1)}, u32[]{:S(2)}, u32[]{:S(2)}) collective-permute-start(f32[1,16,128]{2,1,0:T(8,128)S(1)} %broadcast.92), channel_id=1, source_target_pairs={{0,16},{16,32},{32,48},{48,64},{64,80},{80,96},{96,112},{112,128},... | collective-permute-start | bytes 24584 | tf_op jit(solution)/shard_map/ppermute | solution.py:19
  97.4 219.9 %collective-permute-start.5 = (f32[1,16,128]{2,1,0:T(8,128)S(1)}, f32[1,16,128]{2,1,0:T(8,128)S(1)}, u32[]{:S(2)}, u32[]{:S(2)}) collective-permute-start(f32[1,16,128]{2,1,0:T(8,128)S(1)} %broadcast.92), channel_id=1, source_target_pairs={{16,0},{32,16},{48,32},{64,48},{80,64},{96,80},{112,96},{128,112},... | collective-permute-start | bytes 24584 | tf_op jit(solution)/shard_map/ppermute | solution.py:21
  112.1 9.5 %collective-permute-start.2 = (f32[18,1]{1,0:T(8,128)S(1)}, f32[18,1]{1,0:T(8,128)S(1)}, u32[]{:S(2)}, u32[]{:S(2)}) collective-permute-start(f32[18,1]{1,0:T(8,128)S(1)} %get-tuple-element.56), channel_id=1, source_target_pairs={{0,1},{1,2},{2,3},{3,4},{4,5},{5,6},{6,7},{7,8},{8,9},{9,10},{10,1... | collective-permute-start | bytes 224 | tf_op jit(solution)/shard_map/ppermute | solution.py:19
  309.7 10.2 %collective-permute-start.7 = (f32[1,16,128]{2,1,0:T(8,128)S(1)}, f32[1,16,128]{2,1,0:T(8,128)S(1)}, u32[]{:S(2)}, u32[]{:S(2)}) collective-permute-start(f32[1,16,128]{2,1,0:T(8,128)S(1)} %get-tuple-element.55), channel_id=1, source_target_pairs={{0,16},{16,32},{32,48},{48,64},{64,80},{80,96},{96,112},{112,128},... | collective-permute-start | bytes 24584 | tf_op jit(solution)/shard_map/ppermute | solution.py:19
  311.6 8.3 %collective-permute-start.8 = (f32[1,16,128]{2,1,0:T(8,128)S(1)}, f32[1,16,128]{2,1,0:T(8,128)S(1)}, u32[]{:S(2)}, u32[]{:S(2)}) collective-permute-start(f32[1,16,128]{2,1,0:T(8,128)S(1)} %get-tuple-element.54), channel_id=1, source_target_pairs={{16,0},{32,16},{48,32},{64,48},{80,64},{96,80},{112,96},{128,112},... | collective-permute-start | bytes 24584 | tf_op jit(solution)/shard_map/ppermute | solution.py:21
  317.4 14.0 %collective-permute-start.6 = (f32[18,1,128]{2,1,0:T(1,128)S(1)}, f32[18,1,128]{2,1,0:T(1,128)S(1)}, u32[]{:S(2)}, u32[]{:S(2)}) collective-permute-start(f32[18,1,128]{2,1,0:T(1,128)S(1)} %pad_maximum_fusion.83), channel_id=1, source_target_pairs={{0,1},{1,2},{2,3},{3,4},{4,5},{5,6},{6,7},{7,8},{8,9},{9,10},{10,1... | collective-permute-start | bytes 27656 | tf_op jit(solution)/shard_map/ppermute | solution.py:19
  319.9 11.6 %collective-permute-start.10 = (f32[18,1,128]{2,1,0:T(1,128)S(1)}, f32[18,1,128]{2,1,0:T(1,128)S(1)}, u32[]{:S(2)}, u32[]{:S(2)}) collective-permute-start(f32[18,1,128]{2,1,0:T(1,128)S(1)} %get-tuple-element.43), channel_id=1, source_target_pairs={{0,1},{1,2},{2,3},{3,4},{4,5},{5,6},{6,7},{7,8},{8,9},{9,10},{10,1... | collective-permute-start | bytes 27656 | tf_op jit(solution)/shard_map/ppermute | solution.py:19
  329.5 29.6 %collective-permute-start.18 = (f32[1,16,128]{2,1,0:T(8,128)S(1)}, f32[1,16,128]{2,1,0:T(8,128)S(1)}, u32[]{:S(2)}, u32[]{:S(2)}) collective-permute-start(f32[1,16,128]{2,1,0:T(8,128)S(1)} %slice.550), channel_id=1, source_target_pairs={{0,16},{16,32},{32,48},{48,64},{64,80},{80,96},{96,112},{112,128},... | collective-permute-start | bytes 24584 | tf_op jit(solution)/shard_map/ppermute | solution.py:19
  331.6 15.5 %collective-permute-start.11 = (f32[1,16,128]{2,1,0:T(8,128)S(1)}, f32[1,16,128]{2,1,0:T(8,128)S(1)}, u32[]{:S(2)}, u32[]{:S(2)}) collective-permute-start(f32[1,16,128]{2,1,0:T(8,128)S(1)} %get-tuple-element.30), channel_id=1, source_target_pairs={{0,16},{16,32},{32,48},{48,64},{64,80},{80,96},{96,112},{112,128},... | collective-permute-start | bytes 24584 | tf_op jit(solution)/shard_map/ppermute | solution.py:19
  333.6 13.6 %collective-permute-start.12 = (f32[1,16,128]{2,1,0:T(8,128)S(1)}, f32[1,16,128]{2,1,0:T(8,128)S(1)}, u32[]{:S(2)}, u32[]{:S(2)}) collective-permute-start(f32[1,16,128]{2,1,0:T(8,128)S(1)} %get-tuple-element.31), channel_id=1, source_target_pairs={{16,0},{32,16},{48,32},{64,48},{80,64},{96,80},{112,96},{128,112},... | collective-permute-start | bytes 24584 | tf_op jit(solution)/shard_map/ppermute | solution.py:21
  339.5 12.3 %collective-permute-start.14 = (f32[1,16,128]{2,1,0:T(8,128)S(1)}, f32[1,16,128]{2,1,0:T(8,128)S(1)}, u32[]{:S(2)}, u32[]{:S(2)}) collective-permute-start(f32[1,16,128]{2,1,0:T(8,128)S(1)} %get-tuple-element.53), channel_id=1, source_target_pairs={{0,16},{16,32},{32,48},{48,64},{64,80},{80,96},{96,112},{112,128},... | collective-permute-start | bytes 24584 | tf_op jit(solution)/shard_map/ppermute | solution.py:19
  341.4 10.4 %collective-permute-start.15 = (f32[1,16,128]{2,1,0:T(8,128)S(1)}, f32[1,16,128]{2,1,0:T(8,128)S(1)}, u32[]{:S(2)}, u32[]{:S(2)}) collective-permute-start(f32[1,16,128]{2,1,0:T(8,128)S(1)} %get-tuple-element.52), channel_id=1, source_target_pairs={{16,0},{32,16},{48,32},{64,48},{80,64},{96,80},{112,96},{128,112},... | collective-permute-start | bytes 24584 | tf_op jit(solution)/shard_map/ppermute | solution.py:21
  347.2 14.0 %collective-permute-start.13 = (f32[18,1,128]{2,1,0:T(1,128)S(1)}, f32[18,1,128]{2,1,0:T(1,128)S(1)}, u32[]{:S(2)}, u32[]{:S(2)}) collective-permute-start(f32[18,1,128]{2,1,0:T(1,128)S(1)} %pad_maximum_fusion.78), channel_id=1, source_target_pairs={{0,1},{1,2},{2,3},{3,4},{4,5},{5,6},{6,7},{7,8},{8,9},{9,10},{10,1... | collective-permute-start | bytes 27656 | tf_op jit(solution)/shard_map/ppermute | solution.py:19
  351.8 9.5 %collective-permute-start.16 = (f32[18,1,128]{2,1,0:T(1,128)S(1)}, f32[18,1,128]{2,1,0:T(1,128)S(1)}, u32[]{:S(2)}, u32[]{:S(2)}) collective-permute-start(f32[18,1,128]{2,1,0:T(1,128)S(1)} %get-tuple-element.40), channel_id=1, source_target_pairs={{1,0},{2,1},{3,2},{4,3},{5,4},{6,5},{7,6},{8,7},{9,8},{10,9},{11,1... | collective-permute-start | bytes 27656 | tf_op jit(solution)/shard_map/ppermute | solution.py:21
  356.7 9.2 %collective-permute-start.17 = (f32[18,1,128]{2,1,0:T(1,128)S(1)}, f32[18,1,128]{2,1,0:T(1,128)S(1)}, u32[]{:S(2)}, u32[]{:S(2)}) collective-permute-start(f32[18,1,128]{2,1,0:T(1,128)S(1)} %get-tuple-element.41), channel_id=1, source_target_pairs={{0,1},{1,2},{2,3},{3,4},{4,5},{5,6},{6,7},{7,8},{8,9},{9,10},{10,1... | collective-permute-start | bytes 27656 | tf_op jit(solution)/shard_map/ppermute | solution.py:19
  359.3 33.7 %collective-permute-start.26 = (f32[1,16,128]{2,1,0:T(8,128)S(1)}, f32[1,16,128]{2,1,0:T(8,128)S(1)}, u32[]{:S(2)}, u32[]{:S(2)}) collective-permute-start(f32[1,16,128]{2,1,0:T(8,128)S(1)} %slice.561), channel_id=1, source_target_pairs={{0,16},{16,32},{32,48},{48,64},{64,80},{80,96},{96,112},{112,128},... | collective-permute-start | bytes 24584 | tf_op jit(solution)/shard_map/ppermute | solution.py:19
  366.0 15.5 %collective-permute-start.19 = (f32[1,16,128]{2,1,0:T(8,128)S(1)}, f32[1,16,128]{2,1,0:T(8,128)S(1)}, u32[]{:S(2)}, u32[]{:S(2)}) collective-permute-start(f32[1,16,128]{2,1,0:T(8,128)S(1)} %get-tuple-element.28), channel_id=1, source_target_pairs={{0,16},{16,32},{32,48},{48,64},{64,80},{80,96},{96,112},{112,128},... | collective-permute-start | bytes 24584 | tf_op jit(solution)/shard_map/ppermute | solution.py:19
  368.0 13.5 %collective-permute-start.20 = (f32[1,16,128]{2,1,0:T(8,128)S(1)}, f32[1,16,128]{2,1,0:T(8,128)S(1)}, u32[]{:S(2)}, u32[]{:S(2)}) collective-permute-start(f32[1,16,128]{2,1,0:T(8,128)S(1)} %get-tuple-element.29), channel_id=1, source_target_pairs={{16,0},{32,16},{48,32},{64,48},{80,64},{96,80},{112,96},{128,112},... | collective-permute-start | bytes 24584 | tf_op jit(solution)/shard_map/ppermute | solution.py:21
  373.8 9.7 %collective-permute-start.22 = (f32[1,16,128]{2,1,0:T(8,128)S(1)}, f32[1,16,128]{2,1,0:T(8,128)S(1)}, u32[]{:S(2)}, u32[]{:S(2)}) collective-permute-start(f32[1,16,128]{2,1,0:T(8,128)S(1)} %get-tuple-element.51), channel_id=1, source_target_pairs={{0,16},{16,32},{32,48},{48,64},{64,80},{80,96},{96,112},{112,128},... | collective-permute-start | bytes 24584 | tf_op jit(solution)/shard_map/ppermute | solution.py:19
  375.7 7.7 %collective-permute-start.23 = (f32[1,16,128]{2,1,0:T(8,128)S(1)}, f32[1,16,128]{2,1,0:T(8,128)S(1)}, u32[]{:S(2)}, u32[]{:S(2)}) collective-permute-start(f32[1,16,128]{2,1,0:T(8,128)S(1)} %get-tuple-element.50), channel_id=1, source_target_pairs={{16,0},{32,16},{48,32},{64,48},{80,64},{96,80},{112,96},{128,112},... | collective-permute-start | bytes 24584 | tf_op jit(solution)/shard_map/ppermute | solution.py:21
  381.5 13.5 %collective-permute-start.21 = (f32[18,1,128]{2,1,0:T(1,128)S(1)}, f32[18,1,128]{2,1,0:T(1,128)S(1)}, u32[]{:S(2)}, u32[]{:S(2)}) collective-permute-start(f32[18,1,128]{2,1,0:T(1,128)S(1)} %pad_maximum_fusion.73), channel_id=1, source_target_pairs={{0,1},{1,2},{2,3},{3,4},{4,5},{5,6},{6,7},{7,8},{8,9},{9,10},{10,1... | collective-permute-start | bytes 27656 | tf_op jit(solution)/shard_map/ppermute | solution.py:19
  383.5 11.6 %collective-permute-start.24 = (f32[18,1,128]{2,1,0:T(1,128)S(1)}, f32[18,1,128]{2,1,0:T(1,128)S(1)}, u32[]{:S(2)}, u32[]{:S(2)}) collective-permute-start(f32[18,1,128]{2,1,0:T(1,128)S(1)} %get-tuple-element.38), channel_id=1, source_target_pairs={{1,0},{2,1},{3,2},{4,3},{5,4},{6,5},{7,6},{8,7},{9,8},{10,9},{11,1... | collective-permute-start | bytes 27656 | tf_op jit(solution)/shard_map/ppermute | solution.py:21
  391.1 9.2 %collective-permute-start.25 = (f32[18,1,128]{2,1,0:T(1,128)S(1)}, f32[18,1,128]{2,1,0:T(1,128)S(1)}, u32[]{:S(2)}, u32[]{:S(2)}) collective-permute-start(f32[18,1,128]{2,1,0:T(1,128)S(1)} %get-tuple-element.39), channel_id=1, source_target_pairs={{0,1},{1,2},{2,3},{3,4},{4,5},{5,6},{6,7},{7,8},{8,9},{9,10},{10,1... | collective-permute-start | bytes 27656 | tf_op jit(solution)/shard_map/ppermute | solution.py:19
  393.1 34.2 %collective-permute-start.34 = (f32[1,16,128]{2,1,0:T(8,128)S(1)}, f32[1,16,128]{2,1,0:T(8,128)S(1)}, u32[]{:S(2)}, u32[]{:S(2)}) collective-permute-start(f32[1,16,128]{2,1,0:T(8,128)S(1)} %slice.572), channel_id=1, source_target_pairs={{0,16},{16,32},{32,48},{48,64},{64,80},{80,96},{96,112},{112,128},... | collective-permute-start | bytes 24584 | tf_op jit(solution)/shard_map/ppermute | solution.py:19
  400.4 15.5 %collective-permute-start.27 = (f32[1,16,128]{2,1,0:T(8,128)S(1)}, f32[1,16,128]{2,1,0:T(8,128)S(1)}, u32[]{:S(2)}, u32[]{:S(2)}) collective-permute-start(f32[1,16,128]{2,1,0:T(8,128)S(1)} %get-tuple-element.26), channel_id=1, source_target_pairs={{0,16},{16,32},{32,48},{48,64},{64,80},{80,96},{96,112},{112,128},... | collective-permute-start | bytes 24584 | tf_op jit(solution)/shard_map/ppermute | solution.py:19
  402.3 13.5 %collective-permute-start.28 = (f32[1,16,128]{2,1,0:T(8,128)S(1)}, f32[1,16,128]{2,1,0:T(8,128)S(1)}, u32[]{:S(2)}, u32[]{:S(2)}) collective-permute-start(f32[1,16,128]{2,1,0:T(8,128)S(1)} %get-tuple-element.27), channel_id=1, source_target_pairs={{16,0},{32,16},{48,32},{64,48},{80,64},{96,80},{112,96},{128,112},... | collective-permute-start | bytes 24584 | tf_op jit(solution)/shard_map/ppermute | solution.py:21
  408.1 9.7 %collective-permute-start.30 = (f32[1,16,128]{2,1,0:T(8,128)S(1)}, f32[1,16,128]{2,1,0:T(8,128)S(1)}, u32[]{:S(2)}, u32[]{:S(2)}) collective-permute-start(f32[1,16,128]{2,1,0:T(8,128)S(1)} %get-tuple-element.49), channel_id=1, source_target_pairs={{0,16},{16,32},{32,48},{48,64},{64,80},{80,96},{96,112},{112,128},... | collective-permute-start | bytes 24584 | tf_op jit(solution)/shard_map/ppermute | solution.py:19
  410.1 7.7 %collective-permute-start.31 = (f32[1,16,128]{2,1,0:T(8,128)S(1)}, f32[1,16,128]{2,1,0:T(8,128)S(1)}, u32[]{:S(2)}, u32[]{:S(2)}) collective-permute-start(f32[1,16,128]{2,1,0:T(8,128)S(1)} %get-tuple-element.48), channel_id=1, source_target_pairs={{16,0},{32,16},{48,32},{64,48},{80,64},{96,80},{112,96},{128,112},... | collective-permute-start | bytes 24584 | tf_op jit(solution)/shard_map/ppermute | solution.py:21
  415.9 13.5 %collective-permute-start.29 = (f32[18,1,128]{2,1,0:T(1,128)S(1)}, f32[18,1,128]{2,1,0:T(1,128)S(1)}, u32[]{:S(2)}, u32[]{:S(2)}) collective-permute-start(f32[18,1,128]{2,1,0:T(1,128)S(1)} %pad_maximum_fusion.68), channel_id=1, source_target_pairs={{0,1},{1,2},{2,3},{3,4},{4,5},{5,6},{6,7},{7,8},{8,9},{9,10},{10,1... | collective-permute-start | bytes 27656 | tf_op jit(solution)/shard_map/ppermute | solution.py:19
  417.8 11.6 %collective-permute-start.32 = (f32[18,1,128]{2,1,0:T(1,128)S(1)}, f32[18,1,128]{2,1,0:T(1,128)S(1)}, u32[]{:S(2)}, u32[]{:S(2)}) collective-permute-start(f32[18,1,128]{2,1,0:T(1,128)S(1)} %get-tuple-element.36), channel_id=1, source_target_pairs={{1,0},{2,1},{3,2},{4,3},{5,4},{6,5},{7,6},{8,7},{9,8},{10,9},{11,1... | collective-permute-start | bytes 27656 | tf_op jit(solution)/shard_map/ppermute | solution.py:21
  425.4 9.2 %collective-permute-start.33 = (f32[18,1,128]{2,1,0:T(1,128)S(1)}, f32[18,1,128]{2,1,0:T(1,128)S(1)}, u32[]{:S(2)}, u32[]{:S(2)}) collective-permute-start(f32[18,1,128]{2,1,0:T(1,128)S(1)} %get-tuple-element.37), channel_id=1, source_target_pairs={{0,1},{1,2},{2,3},{3,4},{4,5},{5,6},{6,7},{7,8},{8,9},{9,10},{10,1... | collective-permute-start | bytes 27656 | tf_op jit(solution)/shard_map/ppermute | solution.py:19
  427.5 34.2 %collective-permute-start.42 = (f32[1,16,128]{2,1,0:T(8,128)S(1)}, f32[1,16,128]{2,1,0:T(8,128)S(1)}, u32[]{:S(2)}, u32[]{:S(2)}) collective-permute-start(f32[1,16,128]{2,1,0:T(8,128)S(1)} %slice.583), channel_id=1, source_target_pairs={{0,16},{16,32},{32,48},{48,64},{64,80},{80,96},{96,112},{112,128},... | collective-permute-start | bytes 24584 | tf_op jit(solution)/shard_map/ppermute | solution.py:19
  434.7 15.5 %collective-permute-start.35 = (f32[1,16,128]{2,1,0:T(8,128)S(1)}, f32[1,16,128]{2,1,0:T(8,128)S(1)}, u32[]{:S(2)}, u32[]{:S(2)}) collective-permute-start(f32[1,16,128]{2,1,0:T(8,128)S(1)} %get-tuple-element.24), channel_id=1, source_target_pairs={{0,16},{16,32},{32,48},{48,64},{64,80},{80,96},{96,112},{112,128},... | collective-permute-start | bytes 24584 | tf_op jit(solution)/shard_map/ppermute | solution.py:19
  436.6 13.5 %collective-permute-start.36 = (f32[1,16,128]{2,1,0:T(8,128)S(1)}, f32[1,16,128]{2,1,0:T(8,128)S(1)}, u32[]{:S(2)}, u32[]{:S(2)}) collective-permute-start(f32[1,16,128]{2,1,0:T(8,128)S(1)} %get-tuple-element.25), channel_id=1, source_target_pairs={{16,0},{32,16},{48,32},{64,48},{80,64},{96,80},{112,96},{128,112},... | collective-permute-start | bytes 24584 | tf_op jit(solution)/shard_map/ppermute | solution.py:21
  442.5 9.7 %collective-permute-start.38 = (f32[1,16,128]{2,1,0:T(8,128)S(1)}, f32[1,16,128]{2,1,0:T(8,128)S(1)}, u32[]{:S(2)}, u32[]{:S(2)}) collective-permute-start(f32[1,16,128]{2,1,0:T(8,128)S(1)} %get-tuple-element.47), channel_id=1, source_target_pairs={{0,16},{16,32},{32,48},{48,64},{64,80},{80,96},{96,112},{112,128},... | collective-permute-start | bytes 24584 | tf_op jit(solution)/shard_map/ppermute | solution.py:19
  444.4 7.7 %collective-permute-start.39 = (f32[1,16,128]{2,1,0:T(8,128)S(1)}, f32[1,16,128]{2,1,0:T(8,128)S(1)}, u32[]{:S(2)}, u32[]{:S(2)}) collective-permute-start(f32[1,16,128]{2,1,0:T(8,128)S(1)} %get-tuple-element.46), channel_id=1, source_target_pairs={{16,0},{32,16},{48,32},{64,48},{80,64},{96,80},{112,96},{128,112},... | collective-permute-start | bytes 24584 | tf_op jit(solution)/shard_map/ppermute | solution.py:21
  450.2 13.5 %collective-permute-start.37 = (f32[18,1,128]{2,1,0:T(1,128)S(1)}, f32[18,1,128]{2,1,0:T(1,128)S(1)}, u32[]{:S(2)}, u32[]{:S(2)}) collective-permute-start(f32[18,1,128]{2,1,0:T(1,128)S(1)} %pad_maximum_fusion.63), channel_id=1, source_target_pairs={{0,1},{1,2},{2,3},{3,4},{4,5},{5,6},{6,7},{7,8},{8,9},{9,10},{10,1... | collective-permute-start | bytes 27656 | tf_op jit(solution)/shard_map/ppermute | solution.py:19
  452.2 11.6 %collective-permute-start.40 = (f32[18,1,128]{2,1,0:T(1,128)S(1)}, f32[18,1,128]{2,1,0:T(1,128)S(1)}, u32[]{:S(2)}, u32[]{:S(2)}) collective-permute-start(f32[18,1,128]{2,1,0:T(1,128)S(1)} %get-tuple-element.34), channel_id=1, source_target_pairs={{1,0},{2,1},{3,2},{4,3},{5,4},{6,5},{7,6},{8,7},{9,8},{10,9},{11,1... | collective-permute-start | bytes 27656 | tf_op jit(solution)/shard_map/ppermute | solution.py:21
  459.7 9.2 %collective-permute-start.41 = (f32[18,1,128]{2,1,0:T(1,128)S(1)}, f32[18,1,128]{2,1,0:T(1,128)S(1)}, u32[]{:S(2)}, u32[]{:S(2)}) collective-permute-start(f32[18,1,128]{2,1,0:T(1,128)S(1)} %get-tuple-element.35), channel_id=1, source_target_pairs={{0,1},{1,2},{2,3},{3,4},{4,5},{5,6},{6,7},{7,8},{8,9},{9,10},{10,1... | collective-permute-start | bytes 27656 | tf_op jit(solution)/shard_map/ppermute | solution.py:19
  461.8 34.2 %collective-permute-start.50 = (f32[1,16,128]{2,1,0:T(8,128)S(1)}, f32[1,16,128]{2,1,0:T(8,128)S(1)}, u32[]{:S(2)}, u32[]{:S(2)}) collective-permute-start(f32[1,16,128]{2,1,0:T(8,128)S(1)} %slice.594), channel_id=1, source_target_pairs={{0,16},{16,32},{32,48},{48,64},{64,80},{80,96},{96,112},{112,128},... | collective-permute-start | bytes 24584 | tf_op jit(solution)/shard_map/ppermute | solution.py:19
  469.0 15.5 %collective-permute-start.43 = (f32[1,16,128]{2,1,0:T(8,128)S(1)}, f32[1,16,128]{2,1,0:T(8,128)S(1)}, u32[]{:S(2)}, u32[]{:S(2)}) collective-permute-start(f32[1,16,128]{2,1,0:T(8,128)S(1)} %get-tuple-element.22), channel_id=1, source_target_pairs={{0,16},{16,32},{32,48},{48,64},{64,80},{80,96},{96,112},{112,128},... | collective-permute-start | bytes 24584 | tf_op jit(solution)/shard_map/ppermute | solution.py:19
  470.9 13.5 %collective-permute-start.44 = (f32[1,16,128]{2,1,0:T(8,128)S(1)}, f32[1,16,128]{2,1,0:T(8,128)S(1)}, u32[]{:S(2)}, u32[]{:S(2)}) collective-permute-start(f32[1,16,128]{2,1,0:T(8,128)S(1)} %get-tuple-element.23), channel_id=1, source_target_pairs={{16,0},{32,16},{48,32},{64,48},{80,64},{96,80},{112,96},{128,112},... | collective-permute-start | bytes 24584 | tf_op jit(solution)/shard_map/ppermute | solution.py:21
  476.8 9.7 %collective-permute-start.46 = (f32[1,16,128]{2,1,0:T(8,128)S(1)}, f32[1,16,128]{2,1,0:T(8,128)S(1)}, u32[]{:S(2)}, u32[]{:S(2)}) collective-permute-start(f32[1,16,128]{2,1,0:T(8,128)S(1)} %get-tuple-element.44), channel_id=1, source_target_pairs={{0,16},{16,32},{32,48},{48,64},{64,80},{80,96},{96,112},{112,128},... | collective-permute-start | bytes 24584 | tf_op jit(solution)/shard_map/ppermute | solution.py:19
  484.5 11.6 %collective-permute-start.45 = (f32[18,1,128]{2,1,0:T(1,128)S(1)}, f32[18,1,128]{2,1,0:T(1,128)S(1)}, u32[]{:S(2)}, u32[]{:S(2)}) collective-permute-start(f32[18,1,128]{2,1,0:T(1,128)S(1)} %pad_maximum_fusion.58), channel_id=1, source_target_pairs={{0,1},{1,2},{2,3},{3,4},{4,5},{5,6},{6,7},{7,8},{8,9},{9,10},{10,1... | collective-permute-start | bytes 27656 | tf_op jit(solution)/shard_map/ppermute | solution.py:19
  486.5 9.6 %collective-permute-start.48 = (f32[18,1,128]{2,1,0:T(1,128)S(1)}, f32[18,1,128]{2,1,0:T(1,128)S(1)}, u32[]{:S(2)}, u32[]{:S(2)}) collective-permute-start(f32[18,1,128]{2,1,0:T(1,128)S(1)} %get-tuple-element.32), channel_id=1, source_target_pairs={{1,0},{2,1},{3,2},{4,3},{5,4},{6,5},{7,6},{8,7},{9,8},{10,9},{11,1... | collective-permute-start | bytes 27656 | tf_op jit(solution)/shard_map/ppermute | solution.py:21
  494.0 9.2 %collective-permute-start.49 = (f32[18,1,128]{2,1,0:T(1,128)S(1)}, f32[18,1,128]{2,1,0:T(1,128)S(1)}, u32[]{:S(2)}, u32[]{:S(2)}) collective-permute-start(f32[18,1,128]{2,1,0:T(1,128)S(1)} %get-tuple-element.33), channel_id=1, source_target_pairs={{0,1},{1,2},{2,3},{3,4},{4,5},{5,6},{6,7},{7,8},{8,9},{9,10},{10,1... | collective-permute-start | bytes 27656 | tf_op jit(solution)/shard_map/ppermute | solution.py:19
  (16 other events, 248.5 us)
Sparse Core Ops, SparseCore 0:
  10.2 66.1 all-gather.1
  95.4 213.1 reduce-scatter.1
where the time goes:
time: 513 us; the launch traced here: 511 us
  waiting for transfers between devices  283 us (55%)
  starting transfers between devices  188 us (37%)
  between operations  15.3 us (3%)
  local copies, waits for them, and re-layouts  9.79 us (2%)
  matrix products  9.23 us (2%)
  other arithmetic  5.81 us (1%)
    reduce_scatter x1, waiting for transfers between devices, on_device(): summed = lax.psum_scatter(ordered, 'fault', scatter_dimension=0, tiled=True)  184 us
    ppermute x20, starting transfers between devices, extended(): lax.ppermute(head, axis, [((i + 1) % count, i) for i in range(ends)])  120 us
    ppermute x31, starting transfers between devices, extended(): lax.ppermute(tail, axis, [(i, (i + 1) % count) for i in range(ends)])  68.3 us
    all_gather x1, waiting for transfers between devices, on_device(): gathered = lax.all_gather(slip_rate, 'sea', axis=0, tiled=True)  66.4 us
    ppermute x31, waiting for transfers between devices, extended(): lax.ppermute(tail, axis, [(i, (i + 1) % count) for i in range(ends)])  27.2 us
  transfers between devices with their start and end apart: 53, of which 9 were waited for; matrix products, arithmetic and copies ran while one was open for 1% of the time, Pallas kernels for 0%

commit v1 on v0

--- a/solution.py
+++ b/solution.py
@@ -6,6 +6,11 @@
 STEPS = 6
 gravity_step = 0.7
 height_step = 0.7
+
+
+def swapped_in(x, name, d):
+    repeated = jnp.stack([x] * lax.axis_size(name))
+    return jnp.concatenate(lax.all_to_all(repeated, name, 0, 0), axis=d)
 
 
 def extended(cells, sides, width):
@@ -59,7 +64,7 @@
     members = slip_rate.shape[1]
     leaf_count = brick_y * brick_x * fault_count // leaf_size
     targets = jnp.arange(leaf_count)
-    gathered = lax.all_gather(slip_rate, "sea", axis=0, tiled=True)
+    gathered = swapped_in(slip_rate, "sea", 0)
     leaves = gathered.reshape(-1, leaf_size, members)
     near_slip = leaves[near_cols[0, 0]]
     near_term = jnp.einsum(

time: 513 us -> 476 us (0.928)
  waiting for transfers between devices: 283 us -> 239 us
  starting transfers between devices: 188 us -> 196 us
    all_gather x1 -> x0, waiting for transfers between devices: 66.4 us -> none  [on_device(): gathered = lax.all_gather(slip_rate, 'sea', axis=0, tiled=True)]
    all_to_all x0 -> x1, waiting for transfers between devices: none -> 24 us  [swapped_in(): return jnp.concatenate(lax.all_to_all(repeated, name, 0, 0), axis=d)]
    all_to_all x0 -> x1, starting transfers between devices: none -> 8.3 us  [swapped_in(): return jnp.concatenate(lax.all_to_all(repeated, name, 0, 0), axis=d)]
where the time goes in v1:
time: 476 us; the launch traced here: 474 us
  waiting for transfers between devices  239 us (50%)
  starting transfers between devices  196 us (41%)
  between operations  15.4 us (3%)
  local copies, waits for them, and re-layouts  10.9 us (2%)
  matrix products  8.48 us (2%)
    reduce_scatter x1, waiting for transfers between devices, on_device(): summed = lax.psum_scatter(ordered, 'fault', scatter_dimension=0, tiled=True)  185 us
    ppermute x20, starting transfers between devices, extended(): lax.ppermute(head, axis, [((i + 1) % count, i) for i in range(ends)])  120 us
    ppermute x31, starting transfers between devices, extended(): lax.ppermute(tail, axis, [(i, (i + 1) % count) for i in range(ends)])  68.4 us
    ppermute x31, waiting for transfers between devices, extended(): lax.ppermute(tail, axis, [(i, (i + 1) % count) for i in range(ends)])  27.2 us
    all_to_all x1, waiting for transfers between devices, swapped_in(): return jnp.concatenate(lax.all_to_all(repeated, name, 0, 0), axis=d)  24 us
  transfers between devices with their start and end apart: 53, of which 9 were waited for; matrix products, arithmetic and copies ran while one was open for 1% of the time, Pallas kernels for 0%

profile of v1, /device:TPU:288, one launch (start us, length us, event | category | flops | bytes accessed | tf_op | source)
XLA Modules:
  0.0 474.5 jit_solution(16885931649520270922)
XLA Ops:
  7.2 2.1 stack.2
  9.3 8.3 %all-to-all-start = ((bf16[32,128,128]{2,1,0:T(8,128)(2,1)}), bf16[32,128,128]{2,1,0:T(8,128)(2,1)S(1)}, u32[]{:S(2)}, u32[]{:S(2)}) async-start(bf16[32,128,128]{2,1,0:T(8,128)(2,1)} %stack.2), calls=%async_computation | async-start | bytes 2097152 | tf_op jit(solution)/shard_map/all_to_all | solution.py:13
  17.8 24.0 %all-to-all-done = bf16[32,128,128]{2,1,0:T(8,128)(2,1)S(1)} async-done(((bf16[32,128,128]{2,1,0:T(8,128)(2,1)}), bf16[32,128,128]{2,1,0:T(8,128)(2,1)S(1)}, u32[]{:S(2)}, u32[]{:S(2)}) %all-to-all-start) | async-done | bytes 1048608 | tf_op jit(solution)/shard_map/all_to_all | solution.py:13
  41.8 2.0 gather_fusion.1
  43.8 4.1 fusion.5
  47.9 3.5 copy.17
  55.0 2.0 fusion.2
  57.0 2.0 copy.19
  59.0 2.5 collective-permute-start.4
  61.5 5.2 %collective-permute-start.5 = (f32[1,16,128]{2,1,0:T(8,128)S(1)}, f32[1,16,128]{2,1,0:T(8,128)S(1)}, u32[]{:S(2)}, u32[]{:S(2)}) collective-permute-start(f32[1,16,128]{2,1,0:T(8,128)S(1)} %broadcast.94), channel_id=1, source_target_pairs={{16,0},{32,16},{48,32},{64,48},{80,64},{96,80},{112,96},{128,112},... | collective-permute-start | bytes 24584 | tf_op jit(solution)/shard_map/ppermute | solution.py:26
  68.7 5.8 %collective-permute-start.1 = (f32[1,16]{1,0:T(1,128)S(1)}, f32[1,16]{1,0:T(1,128)S(1)}, u32[]{:S(2)}, u32[]{:S(2)}) collective-permute-start(f32[1,16]{1,0:T(1,128)S(1)} %get-tuple-element.58), channel_id=1, source_target_pairs={{16,0},{32,16},{48,32},{64,48},{80,64},{96,80},{112,96},{128,112},... | collective-permute-start | bytes 200 | tf_op jit(solution)/shard_map/ppermute | solution.py:26
  75.8 4.6 collective-permute-start.2
  80.4 4.8 %collective-permute-start.3 = (f32[18,1]{1,0:T(8,128)S(1)}, f32[18,1]{1,0:T(8,128)S(1)}, u32[]{:S(2)}, u32[]{:S(2)}) collective-permute-start(f32[18,1]{1,0:T(8,128)S(1)} %get-tuple-element.57), channel_id=1, source_target_pairs={{1,0},{2,1},{3,2},{4,3},{5,4},{6,5},{7,6},{8,7},{9,8},{10,9},{11,1... | collective-permute-start | bytes 224 | tf_op jit(solution)/shard_map/ppermute | solution.py:26
  85.3 2.2 collective-permute-done.3
  87.6 184.6 %reduce-scatter.2.cloned.1.call-done = f32[1,16,16,128]{3,2,1,0:T(8,128)} async-done(((f32[16,16,16,128]{3,2,1,0:T(8,128)}), f32[1,16,16,128]{3,2,1,0:T(8,128)}) %reduce-scatter.2.cloned.1.call-update) | async-done | bytes 131088 | tf_op jit(solution)/shard_map/reduce_scatter | solution.py:90
  273.3 1.9 collective-permute-start.7
  275.2 5.8 %collective-permute-start.8 = (f32[1,16,128]{2,1,0:T(8,128)S(1)}, f32[1,16,128]{2,1,0:T(8,128)S(1)}, u32[]{:S(2)}, u32[]{:S(2)}) collective-permute-start(f32[1,16,128]{2,1,0:T(8,128)S(1)} %get-tuple-element.54), channel_id=1, source_target_pairs={{16,0},{32,16},{48,32},{64,48},{80,64},{96,80},{112,96},{128,112},... | collective-permute-start | bytes 24584 | tf_op jit(solution)/shard_map/ppermute | solution.py:26
  281.1 2.5 collective-permute-start.6
  283.6 3.8 collective-permute-start.10
  287.4 5.6 %collective-permute-start.9 = (f32[18,1,128]{2,1,0:T(1,128)S(1)}, f32[18,1,128]{2,1,0:T(1,128)S(1)}, u32[]{:S(2)}, u32[]{:S(2)}) collective-permute-start(f32[18,1,128]{2,1,0:T(1,128)S(1)} %get-tuple-element.42), channel_id=1, source_target_pairs={{1,0},{2,1},{3,2},{4,3},{5,4},{6,5},{7,6},{8,7},{9,8},{10,9},{11,1... | collective-permute-start | bytes 27656 | tf_op jit(solution)/shard_map/ppermute | solution.py:26
  297.2 5.8 %collective-permute-start.12 = (f32[1,16,128]{2,1,0:T(8,128)S(1)}, f32[1,16,128]{2,1,0:T(8,128)S(1)}, u32[]{:S(2)}, u32[]{:S(2)}) collective-permute-start(f32[1,16,128]{2,1,0:T(8,128)S(1)} %get-tuple-element.31), channel_id=1, source_target_pairs={{16,0},{32,16},{48,32},{64,48},{80,64},{96,80},{112,96},{128,112},... | collective-permute-start | bytes 24584 | tf_op jit(solution)/shard_map/ppermute | solution.py:26
  305.1 5.8 %collective-permute-start.15 = (f32[1,16,128]{2,1,0:T(8,128)S(1)}, f32[1,16,128]{2,1,0:T(8,128)S(1)}, u32[]{:S(2)}, u32[]{:S(2)}) collective-permute-start(f32[1,16,128]{2,1,0:T(8,128)S(1)} %get-tuple-element.52), channel_id=1, source_target_pairs={{16,0},{32,16},{48,32},{64,48},{80,64},{96,80},{112,96},{128,112},... | collective-permute-start | bytes 24584 | tf_op jit(solution)/shard_map/ppermute | solution.py:26
  310.9 4.5 collective-permute-start.13
  315.4 5.0 %collective-permute-start.16 = (f32[18,1,128]{2,1,0:T(1,128)S(1)}, f32[18,1,128]{2,1,0:T(1,128)S(1)}, u32[]{:S(2)}, u32[]{:S(2)}) collective-permute-start(f32[18,1,128]{2,1,0:T(1,128)S(1)} %get-tuple-element.40), channel_id=1, source_target_pairs={{1,0},{2,1},{3,2},{4,3},{5,4},{6,5},{7,6},{8,7},{9,8},{10,9},{11,1... | collective-permute-start | bytes 27656 | tf_op jit(solution)/shard_map/ppermute | solution.py:26
  320.4 2.4 collective-permute-start.17
  324.9 4.7 collective-permute-done.17
  329.7 1.9 collective-permute-start.19
  331.6 5.8 %collective-permute-start.20 = (f32[1,16,128]{2,1,0:T(8,128)S(1)}, f32[1,16,128]{2,1,0:T(8,128)S(1)}, u32[]{:S(2)}, u32[]{:S(2)}) collective-permute-start(f32[1,16,128]{2,1,0:T(8,128)S(1)} %get-tuple-element.29), channel_id=1, source_target_pairs={{16,0},{32,16},{48,32},{64,48},{80,64},{96,80},{112,96},{128,112},... | collective-permute-start | bytes 24584 | tf_op jit(solution)/shard_map/ppermute | solution.py:26
  339.4 5.8 %collective-permute-start.23 = (f32[1,16,128]{2,1,0:T(8,128)S(1)}, f32[1,16,128]{2,1,0:T(8,128)S(1)}, u32[]{:S(2)}, u32[]{:S(2)}) collective-permute-start(f32[1,16,128]{2,1,0:T(8,128)S(1)} %get-tuple-element.50), channel_id=1, source_target_pairs={{16,0},{32,16},{48,32},{64,48},{80,64},{96,80},{112,96},{128,112},... | collective-permute-start | bytes 24584 | tf_op jit(solution)/shard_map/ppermute | solution.py:26
  345.2 1.9 collective-permute-start.21
  347.1 7.5 %collective-permute-start.24 = (f32[18,1,128]{2,1,0:T(1,128)S(1)}, f32[18,1,128]{2,1,0:T(1,128)S(1)}, u32[]{:S(2)}, u32[]{:S(2)}) collective-permute-start(f32[18,1,128]{2,1,0:T(1,128)S(1)} %get-tuple-element.38), channel_id=1, source_target_pairs={{1,0},{2,1},{3,2},{4,3},{5,4},{6,5},{7,6},{8,7},{9,8},{10,9},{11,1... | collective-permute-start | bytes 27656 | tf_op jit(solution)/shard_map/ppermute | solution.py:26
  358.7 5.1 %collective-permute-done.25 = f32[18,1,128]{2,1,0:T(1,128)S(1)} collective-permute-done((f32[18,1,128]{2,1,0:T(1,128)S(1)}, f32[18,1,128]{2,1,0:T(1,128)S(1)}, u32[]{:S(2)}, u32[]{:S(2)}) %collective-permute-start.25) | collective-permute-done | bytes 9248 | tf_op jit(solution)/shard_map/ppermute | solution.py:24
  364.0 1.9 collective-permute-start.27
  365.9 5.8 %collective-permute-start.28 = (f32[1,16,128]{2,1,0:T(8,128)S(1)}, f32[1,16,128]{2,1,0:T(8,128)S(1)}, u32[]{:S(2)}, u32[]{:S(2)}) collective-permute-start(f32[1,16,128]{2,1,0:T(8,128)S(1)} %get-tuple-element.27), channel_id=1, source_target_pairs={{16,0},{32,16},{48,32},{64,48},{80,64},{96,80},{112,96},{128,112},... | collective-permute-start | bytes 24584 | tf_op jit(solution)/shard_map/ppermute | solution.py:26
  373.7 5.8 %collective-permute-start.31 = (f32[1,16,128]{2,1,0:T(8,128)S(1)}, f32[1,16,128]{2,1,0:T(8,128)S(1)}, u32[]{:S(2)}, u32[]{:S(2)}) collective-permute-start(f32[1,16,128]{2,1,0:T(8,128)S(1)} %get-tuple-element.48), channel_id=1, source_target_pairs={{16,0},{32,16},{48,32},{64,48},{80,64},{96,80},{112,96},{128,112},... | collective-permute-start | bytes 24584 | tf_op jit(solution)/shard_map/ppermute | solution.py:26
  379.5 1.9 collective-permute-start.29
  381.5 7.5 %collective-permute-start.32 = (f32[18,1,128]{2,1,0:T(1,128)S(1)}, f32[18,1,128]{2,1,0:T(1,128)S(1)}, u32[]{:S(2)}, u32[]{:S(2)}) collective-permute-start(f32[18,1,128]{2,1,0:T(1,128)S(1)} %get-tuple-element.36), channel_id=1, source_target_pairs={{1,0},{2,1},{3,2},{4,3},{5,4},{6,5},{7,6},{8,7},{9,8},{10,9},{11,1... | collective-permute-start | bytes 27656 | tf_op jit(solution)/shard_map/ppermute | solution.py:26
  393.0 5.1 %collective-permute-done.33 = f32[18,1,128]{2,1,0:T(1,128)S(1)} collective-permute-done((f32[18,1,128]{2,1,0:T(1,128)S(1)}, f32[18,1,128]{2,1,0:T(1,128)S(1)}, u32[]{:S(2)}, u32[]{:S(2)}) %collective-permute-start.33) | collective-permute-done | bytes 9248 | tf_op jit(solution)/shard_map/ppermute | solution.py:24
  398.3 1.9 collective-permute-start.35
  400.2 5.8 %collective-permute-start.36 = (f32[1,16,128]{2,1,0:T(8,128)S(1)}, f32[1,16,128]{2,1,0:T(8,128)S(1)}, u32[]{:S(2)}, u32[]{:S(2)}) collective-permute-start(f32[1,16,128]{2,1,0:T(8,128)S(1)} %get-tuple-element.25), channel_id=1, source_target_pairs={{16,0},{32,16},{48,32},{64,48},{80,64},{96,80},{112,96},{128,112},... | collective-permute-start | bytes 24584 | tf_op jit(solution)/shard_map/ppermute | solution.py:26
  408.0 5.8 %collective-permute-start.39 = (f32[1,16,128]{2,1,0:T(8,128)S(1)}, f32[1,16,128]{2,1,0:T(8,128)S(1)}, u32[]{:S(2)}, u32[]{:S(2)}) collective-permute-start(f32[1,16,128]{2,1,0:T(8,128)S(1)} %get-tuple-element.46), channel_id=1, source_target_pairs={{16,0},{32,16},{48,32},{64,48},{80,64},{96,80},{112,96},{128,112},... | collective-permute-start | bytes 24584 | tf_op jit(solution)/shard_map/ppermute | solution.py:26
  413.8 1.9 collective-permute-start.37
  415.8 7.5 %collective-permute-start.40 = (f32[18,1,128]{2,1,0:T(1,128)S(1)}, f32[18,1,128]{2,1,0:T(1,128)S(1)}, u32[]{:S(2)}, u32[]{:S(2)}) collective-permute-start(f32[18,1,128]{2,1,0:T(1,128)S(1)} %get-tuple-element.34), channel_id=1, source_target_pairs={{1,0},{2,1},{3,2},{4,3},{5,4},{6,5},{7,6},{8,7},{9,8},{10,9},{11,1... | collective-permute-start | bytes 27656 | tf_op jit(solution)/shard_map/ppermute | solution.py:26
  427.4 5.1 %collective-permute-done.41 = f32[18,1,128]{2,1,0:T(1,128)S(1)} collective-permute-done((f32[18,1,128]{2,1,0:T(1,128)S(1)}, f32[18,1,128]{2,1,0:T(1,128)S(1)}, u32[]{:S(2)}, u32[]{:S(2)}) %collective-permute-start.41) | collective-permute-done | bytes 9248 | tf_op jit(solution)/shard_map/ppermute | solution.py:24
  434.6 5.8 %collective-permute-start.44 = (f32[1,16,128]{2,1,0:T(8,128)S(1)}, f32[1,16,128]{2,1,0:T(8,128)S(1)}, u32[]{:S(2)}, u32[]{:S(2)}) collective-permute-start(f32[1,16,128]{2,1,0:T(8,128)S(1)} %get-tuple-element.23), channel_id=1, source_target_pairs={{16,0},{32,16},{48,32},{64,48},{80,64},{96,80},{112,96},{128,112},... | collective-permute-start | bytes 24584 | tf_op jit(solution)/shard_map/ppermute | solution.py:26
  442.3 5.8 %collective-permute-start.47 = (f32[1,16,128]{2,1,0:T(8,128)S(1)}, f32[1,16,128]{2,1,0:T(8,128)S(1)}, u32[]{:S(2)}, u32[]{:S(2)}) collective-permute-start(f32[1,16,128]{2,1,0:T(8,128)S(1)} %get-tuple-element.45), channel_id=1, source_target_pairs={{16,0},{32,16},{48,32},{64,48},{80,64},{96,80},{112,96},{128,112},... | collective-permute-start | bytes 24584 | tf_op jit(solution)/shard_map/ppermute | solution.py:26
  450.1 7.5 %collective-permute-start.48 = (f32[18,1,128]{2,1,0:T(1,128)S(1)}, f32[18,1,128]{2,1,0:T(1,128)S(1)}, u32[]{:S(2)}, u32[]{:S(2)}) collective-permute-start(f32[18,1,128]{2,1,0:T(1,128)S(1)} %get-tuple-element.32), channel_id=1, source_target_pairs={{1,0},{2,1},{3,2},{4,3},{5,4},{6,5},{7,6},{8,7},{9,8},{10,9},{11,1... | collective-permute-start | bytes 27656 | tf_op jit(solution)/shard_map/ppermute | solution.py:26
  459.7 7.1 %collective-permute-done.49 = f32[18,1,128]{2,1,0:T(1,128)S(1)} collective-permute-done((f32[18,1,128]{2,1,0:T(1,128)S(1)}, f32[18,1,128]{2,1,0:T(1,128)S(1)}, u32[]{:S(2)}, u32[]{:S(2)}) %collective-permute-start.49) | collective-permute-done | bytes 9248 | tf_op jit(solution)/shard_map/ppermute | solution.py:24
  (168 shorter events, 43.7 us)
Async XLA Ops:
  9.3 32.5 %all-to-all-start = ((bf16[32,128,128]{2,1,0:T(8,128)(2,1)}), bf16[32,128,128]{2,1,0:T(8,128)(2,1)S(1)}, u32[]{:S(2)}, u32[]{:S(2)}) async-start(bf16[32,128,128]{2,1,0:T(8,128)(2,1)} %stack.2), calls=%async_computation | async-start | bytes 2097152 | tf_op jit(solution)/shard_map/all_to_all | solution.py:13
  17.6 254.6 %reduce-scatter.2.cloned.1.call-start = ((), (), s32[]{:S(2)}) async-start(), calls=%async_computation.2 | async-start | bytes 2228224 | tf_op jit(solution)/shard_map/reduce_scatter | solution.py:90
  59.0 222.0 %collective-permute-start.4 = (f32[1,16,128]{2,1,0:T(8,128)S(1)}, f32[1,16,128]{2,1,0:T(8,128)S(1)}, u32[]{:S(2)}, u32[]{:S(2)}) collective-permute-start(f32[1,16,128]{2,1,0:T(8,128)S(1)} %broadcast.94), channel_id=1, source_target_pairs={{0,16},{16,32},{32,48},{48,64},{64,80},{80,96},{96,112},{112,128},... | collective-permute-start | bytes 24584 | tf_op jit(solution)/shard_map/ppermute | solution.py:24
  61.5 219.5 %collective-permute-start.5 = (f32[1,16,128]{2,1,0:T(8,128)S(1)}, f32[1,16,128]{2,1,0:T(8,128)S(1)}, u32[]{:S(2)}, u32[]{:S(2)}) collective-permute-start(f32[1,16,128]{2,1,0:T(8,128)S(1)} %broadcast.94), channel_id=1, source_target_pairs={{16,0},{32,16},{48,32},{64,48},{80,64},{96,80},{112,96},{128,112},... | collective-permute-start | bytes 24584 | tf_op jit(solution)/shard_map/ppermute | solution.py:26
  75.8 9.5 %collective-permute-start.2 = (f32[18,1]{1,0:T(8,128)S(1)}, f32[18,1]{1,0:T(8,128)S(1)}, u32[]{:S(2)}, u32[]{:S(2)}) collective-permute-start(f32[18,1]{1,0:T(8,128)S(1)} %get-tuple-element.56), channel_id=1, source_target_pairs={{0,1},{1,2},{2,3},{3,4},{4,5},{5,6},{6,7},{7,8},{8,9},{9,10},{10,1... | collective-permute-start | bytes 224 | tf_op jit(solution)/shard_map/ppermute | solution.py:24
  273.3 10.2 %collective-permute-start.7 = (f32[1,16,128]{2,1,0:T(8,128)S(1)}, f32[1,16,128]{2,1,0:T(8,128)S(1)}, u32[]{:S(2)}, u32[]{:S(2)}) collective-permute-start(f32[1,16,128]{2,1,0:T(8,128)S(1)} %get-tuple-element.55), channel_id=1, source_target_pairs={{0,16},{16,32},{32,48},{48,64},{64,80},{80,96},{96,112},{112,128},... | collective-permute-start | bytes 24584 | tf_op jit(solution)/shard_map/ppermute | solution.py:24
  275.2 8.3 %collective-permute-start.8 = (f32[1,16,128]{2,1,0:T(8,128)S(1)}, f32[1,16,128]{2,1,0:T(8,128)S(1)}, u32[]{:S(2)}, u32[]{:S(2)}) collective-permute-start(f32[1,16,128]{2,1,0:T(8,128)S(1)} %get-tuple-element.54), channel_id=1, source_target_pairs={{16,0},{32,16},{48,32},{64,48},{80,64},{96,80},{112,96},{128,112},... | collective-permute-start | bytes 24584 | tf_op jit(solution)/shard_map/ppermute | solution.py:26
  281.1 14.1 %collective-permute-start.6 = (f32[18,1,128]{2,1,0:T(1,128)S(1)}, f32[18,1,128]{2,1,0:T(1,128)S(1)}, u32[]{:S(2)}, u32[]{:S(2)}) collective-permute-start(f32[18,1,128]{2,1,0:T(1,128)S(1)} %pad_maximum_fusion.83), channel_id=1, source_target_pairs={{0,1},{1,2},{2,3},{3,4},{4,5},{5,6},{6,7},{7,8},{8,9},{9,10},{10,1... | collective-permute-start | bytes 27656 | tf_op jit(solution)/shard_map/ppermute | solution.py:24
  283.6 11.6 %collective-permute-start.10 = (f32[18,1,128]{2,1,0:T(1,128)S(1)}, f32[18,1,128]{2,1,0:T(1,128)S(1)}, u32[]{:S(2)}, u32[]{:S(2)}) collective-permute-start(f32[18,1,128]{2,1,0:T(1,128)S(1)} %get-tuple-element.43), channel_id=1, source_target_pairs={{0,1},{1,2},{2,3},{3,4},{4,5},{5,6},{6,7},{7,8},{8,9},{9,10},{10,1... | collective-permute-start | bytes 27656 | tf_op jit(solution)/shard_map/ppermute | solution.py:24
  293.2 29.6 %collective-permute-start.18 = (f32[1,16,128]{2,1,0:T(8,128)S(1)}, f32[1,16,128]{2,1,0:T(8,128)S(1)}, u32[]{:S(2)}, u32[]{:S(2)}) collective-permute-start(f32[1,16,128]{2,1,0:T(8,128)S(1)} %slice.550), channel_id=1, source_target_pairs={{0,16},{16,32},{32,48},{48,64},{64,80},{80,96},{96,112},{112,128},... | collective-permute-start | bytes 24584 | tf_op jit(solution)/shard_map/ppermute | solution.py:24
  295.3 15.5 %collective-permute-start.11 = (f32[1,16,128]{2,1,0:T(8,128)S(1)}, f32[1,16,128]{2,1,0:T(8,128)S(1)}, u32[]{:S(2)}, u32[]{:S(2)}) collective-permute-start(f32[1,16,128]{2,1,0:T(8,128)S(1)} %get-tuple-element.30), channel_id=1, source_target_pairs={{0,16},{16,32},{32,48},{48,64},{64,80},{80,96},{96,112},{112,128},... | collective-permute-start | bytes 24584 | tf_op jit(solution)/shard_map/ppermute | solution.py:24
  297.2 13.6 %collective-permute-start.12 = (f32[1,16,128]{2,1,0:T(8,128)S(1)}, f32[1,16,128]{2,1,0:T(8,128)S(1)}, u32[]{:S(2)}, u32[]{:S(2)}) collective-permute-start(f32[1,16,128]{2,1,0:T(8,128)S(1)} %get-tuple-element.31), channel_id=1, source_target_pairs={{16,0},{32,16},{48,32},{64,48},{80,64},{96,80},{112,96},{128,112},... | collective-permute-start | bytes 24584 | tf_op jit(solution)/shard_map/ppermute | solution.py:26
  303.1 12.2 %collective-permute-start.14 = (f32[1,16,128]{2,1,0:T(8,128)S(1)}, f32[1,16,128]{2,1,0:T(8,128)S(1)}, u32[]{:S(2)}, u32[]{:S(2)}) collective-permute-start(f32[1,16,128]{2,1,0:T(8,128)S(1)} %get-tuple-element.53), channel_id=1, source_target_pairs={{0,16},{16,32},{32,48},{48,64},{64,80},{80,96},{96,112},{112,128},... | collective-permute-start | bytes 24584 | tf_op jit(solution)/shard_map/ppermute | solution.py:24
  305.1 10.3 %collective-permute-start.15 = (f32[1,16,128]{2,1,0:T(8,128)S(1)}, f32[1,16,128]{2,1,0:T(8,128)S(1)}, u32[]{:S(2)}, u32[]{:S(2)}) collective-permute-start(f32[1,16,128]{2,1,0:T(8,128)S(1)} %get-tuple-element.52), channel_id=1, source_target_pairs={{16,0},{32,16},{48,32},{64,48},{80,64},{96,80},{112,96},{128,112},... | collective-permute-start | bytes 24584 | tf_op jit(solution)/shard_map/ppermute | solution.py:26
  310.9 14.0 %collective-permute-start.13 = (f32[18,1,128]{2,1,0:T(1,128)S(1)}, f32[18,1,128]{2,1,0:T(1,128)S(1)}, u32[]{:S(2)}, u32[]{:S(2)}) collective-permute-start(f32[18,1,128]{2,1,0:T(1,128)S(1)} %pad_maximum_fusion.78), channel_id=1, source_target_pairs={{0,1},{1,2},{2,3},{3,4},{4,5},{5,6},{6,7},{7,8},{8,9},{9,10},{10,1... | collective-permute-start | bytes 27656 | tf_op jit(solution)/shard_map/ppermute | solution.py:24
  315.4 9.5 %collective-permute-start.16 = (f32[18,1,128]{2,1,0:T(1,128)S(1)}, f32[18,1,128]{2,1,0:T(1,128)S(1)}, u32[]{:S(2)}, u32[]{:S(2)}) collective-permute-start(f32[18,1,128]{2,1,0:T(1,128)S(1)} %get-tuple-element.40), channel_id=1, source_target_pairs={{1,0},{2,1},{3,2},{4,3},{5,4},{6,5},{7,6},{8,7},{9,8},{10,9},{11,1... | collective-permute-start | bytes 27656 | tf_op jit(solution)/shard_map/ppermute | solution.py:26
  320.4 9.2 %collective-permute-start.17 = (f32[18,1,128]{2,1,0:T(1,128)S(1)}, f32[18,1,128]{2,1,0:T(1,128)S(1)}, u32[]{:S(2)}, u32[]{:S(2)}) collective-permute-start(f32[18,1,128]{2,1,0:T(1,128)S(1)} %get-tuple-element.41), channel_id=1, source_target_pairs={{0,1},{1,2},{2,3},{3,4},{4,5},{5,6},{6,7},{7,8},{8,9},{9,10},{10,1... | collective-permute-start | bytes 27656 | tf_op jit(solution)/shard_map/ppermute | solution.py:24
  322.9 33.7 %collective-permute-start.26 = (f32[1,16,128]{2,1,0:T(8,128)S(1)}, f32[1,16,128]{2,1,0:T(8,128)S(1)}, u32[]{:S(2)}, u32[]{:S(2)}) collective-permute-start(f32[1,16,128]{2,1,0:T(8,128)S(1)} %slice.561), channel_id=1, source_target_pairs={{0,16},{16,32},{32,48},{48,64},{64,80},{80,96},{96,112},{112,128},... | collective-permute-start | bytes 24584 | tf_op jit(solution)/shard_map/ppermute | solution.py:24
  329.7 15.5 %collective-permute-start.19 = (f32[1,16,128]{2,1,0:T(8,128)S(1)}, f32[1,16,128]{2,1,0:T(8,128)S(1)}, u32[]{:S(2)}, u32[]{:S(2)}) collective-permute-start(f32[1,16,128]{2,1,0:T(8,128)S(1)} %get-tuple-element.28), channel_id=1, source_target_pairs={{0,16},{16,32},{32,48},{48,64},{64,80},{80,96},{96,112},{112,128},... | collective-permute-start | bytes 24584 | tf_op jit(solution)/shard_map/ppermute | solution.py:24
  331.6 13.5 %collective-permute-start.20 = (f32[1,16,128]{2,1,0:T(8,128)S(1)}, f32[1,16,128]{2,1,0:T(8,128)S(1)}, u32[]{:S(2)}, u32[]{:S(2)}) collective-permute-start(f32[1,16,128]{2,1,0:T(8,128)S(1)} %get-tuple-element.29), channel_id=1, source_target_pairs={{16,0},{32,16},{48,32},{64,48},{80,64},{96,80},{112,96},{128,112},... | collective-permute-start | bytes 24584 | tf_op jit(solution)/shard_map/ppermute | solution.py:26
  337.4 9.7 %collective-permute-start.22 = (f32[1,16,128]{2,1,0:T(8,128)S(1)}, f32[1,16,128]{2,1,0:T(8,128)S(1)}, u32[]{:S(2)}, u32[]{:S(2)}) collective-permute-start(f32[1,16,128]{2,1,0:T(8,128)S(1)} %get-tuple-element.51), channel_id=1, source_target_pairs={{0,16},{16,32},{32,48},{48,64},{64,80},{80,96},{96,112},{112,128},... | collective-permute-start | bytes 24584 | tf_op jit(solution)/shard_map/ppermute | solution.py:24
  339.4 7.7 %collective-permute-start.23 = (f32[1,16,128]{2,1,0:T(8,128)S(1)}, f32[1,16,128]{2,1,0:T(8,128)S(1)}, u32[]{:S(2)}, u32[]{:S(2)}) collective-permute-start(f32[1,16,128]{2,1,0:T(8,128)S(1)} %get-tuple-element.50), channel_id=1, source_target_pairs={{16,0},{32,16},{48,32},{64,48},{80,64},{96,80},{112,96},{128,112},... | collective-permute-start | bytes 24584 | tf_op jit(solution)/shard_map/ppermute | solution.py:26
  345.2 13.5 %collective-permute-start.21 = (f32[18,1,128]{2,1,0:T(1,128)S(1)}, f32[18,1,128]{2,1,0:T(1,128)S(1)}, u32[]{:S(2)}, u32[]{:S(2)}) collective-permute-start(f32[18,1,128]{2,1,0:T(1,128)S(1)} %pad_maximum_fusion.73), channel_id=1, source_target_pairs={{0,1},{1,2},{2,3},{3,4},{4,5},{5,6},{6,7},{7,8},{8,9},{9,10},{10,1... | collective-permute-start | bytes 27656 | tf_op jit(solution)/shard_map/ppermute | solution.py:24
  347.1 11.6 %collective-permute-start.24 = (f32[18,1,128]{2,1,0:T(1,128)S(1)}, f32[18,1,128]{2,1,0:T(1,128)S(1)}, u32[]{:S(2)}, u32[]{:S(2)}) collective-permute-start(f32[18,1,128]{2,1,0:T(1,128)S(1)} %get-tuple-element.38), channel_id=1, source_target_pairs={{1,0},{2,1},{3,2},{4,3},{5,4},{6,5},{7,6},{8,7},{9,8},{10,9},{11,1... | collective-permute-start | bytes 27656 | tf_op jit(solution)/shard_map/ppermute | solution.py:26
  354.7 9.2 %collective-permute-start.25 = (f32[18,1,128]{2,1,0:T(1,128)S(1)}, f32[18,1,128]{2,1,0:T(1,128)S(1)}, u32[]{:S(2)}, u32[]{:S(2)}) collective-permute-start(f32[18,1,128]{2,1,0:T(1,128)S(1)} %get-tuple-element.39), channel_id=1, source_target_pairs={{0,1},{1,2},{2,3},{3,4},{4,5},{5,6},{6,7},{7,8},{8,9},{9,10},{10,1... | collective-permute-start | bytes 27656 | tf_op jit(solution)/shard_map/ppermute | solution.py:24
  356.8 34.2 %collective-permute-start.34 = (f32[1,16,128]{2,1,0:T(8,128)S(1)}, f32[1,16,128]{2,1,0:T(8,128)S(1)}, u32[]{:S(2)}, u32[]{:S(2)}) collective-permute-start(f32[1,16,128]{2,1,0:T(8,128)S(1)} %slice.572), channel_id=1, source_target_pairs={{0,16},{16,32},{32,48},{48,64},{64,80},{80,96},{96,112},{112,128},... | collective-permute-start | bytes 24584 | tf_op jit(solution)/shard_map/ppermute | solution.py:24
  364.0 15.5 %collective-permute-start.27 = (f32[1,16,128]{2,1,0:T(8,128)S(1)}, f32[1,16,128]{2,1,0:T(8,128)S(1)}, u32[]{:S(2)}, u32[]{:S(2)}) collective-permute-start(f32[1,16,128]{2,1,0:T(8,128)S(1)} %get-tuple-element.26), channel_id=1, source_target_pairs={{0,16},{16,32},{32,48},{48,64},{64,80},{80,96},{96,112},{112,128},... | collective-permute-start | bytes 24584 | tf_op jit(solution)/shard_map/ppermute | solution.py:24
  365.9 13.5 %collective-permute-start.28 = (f32[1,16,128]{2,1,0:T(8,128)S(1)}, f32[1,16,128]{2,1,0:T(8,128)S(1)}, u32[]{:S(2)}, u32[]{:S(2)}) collective-permute-start(f32[1,16,128]{2,1,0:T(8,128)S(1)} %get-tuple-element.27), channel_id=1, source_target_pairs={{16,0},{32,16},{48,32},{64,48},{80,64},{96,80},{112,96},{128,112},... | collective-permute-start | bytes 24584 | tf_op jit(solution)/shard_map/ppermute | solution.py:26
  371.8 9.7 %collective-permute-start.30 = (f32[1,16,128]{2,1,0:T(8,128)S(1)}, f32[1,16,128]{2,1,0:T(8,128)S(1)}, u32[]{:S(2)}, u32[]{:S(2)}) collective-permute-start(f32[1,16,128]{2,1,0:T(8,128)S(1)} %get-tuple-element.49), channel_id=1, source_target_pairs={{0,16},{16,32},{32,48},{48,64},{64,80},{80,96},{96,112},{112,128},... | collective-permute-start | bytes 24584 | tf_op jit(solution)/shard_map/ppermute | solution.py:24
  373.7 7.7 %collective-permute-start.31 = (f32[1,16,128]{2,1,0:T(8,128)S(1)}, f32[1,16,128]{2,1,0:T(8,128)S(1)}, u32[]{:S(2)}, u32[]{:S(2)}) collective-permute-start(f32[1,16,128]{2,1,0:T(8,128)S(1)} %get-tuple-element.48), channel_id=1, source_target_pairs={{16,0},{32,16},{48,32},{64,48},{80,64},{96,80},{112,96},{128,112},... | collective-permute-start | bytes 24584 | tf_op jit(solution)/shard_map/ppermute | solution.py:26
  379.5 13.5 %collective-permute-start.29 = (f32[18,1,128]{2,1,0:T(1,128)S(1)}, f32[18,1,128]{2,1,0:T(1,128)S(1)}, u32[]{:S(2)}, u32[]{:S(2)}) collective-permute-start(f32[18,1,128]{2,1,0:T(1,128)S(1)} %pad_maximum_fusion.68), channel_id=1, source_target_pairs={{0,1},{1,2},{2,3},{3,4},{4,5},{5,6},{6,7},{7,8},{8,9},{9,10},{10,1... | collective-permute-start | bytes 27656 | tf_op jit(solution)/shard_map/ppermute | solution.py:24
  381.5 11.6 %collective-permute-start.32 = (f32[18,1,128]{2,1,0:T(1,128)S(1)}, f32[18,1,128]{2,1,0:T(1,128)S(1)}, u32[]{:S(2)}, u32[]{:S(2)}) collective-permute-start(f32[18,1,128]{2,1,0:T(1,128)S(1)} %get-tuple-element.36), channel_id=1, source_target_pairs={{1,0},{2,1},{3,2},{4,3},{5,4},{6,5},{7,6},{8,7},{9,8},{10,9},{11,1... | collective-permute-start | bytes 27656 | tf_op jit(solution)/shard_map/ppermute | solution.py:26
  389.0 9.2 %collective-permute-start.33 = (f32[18,1,128]{2,1,0:T(1,128)S(1)}, f32[18,1,128]{2,1,0:T(1,128)S(1)}, u32[]{:S(2)}, u32[]{:S(2)}) collective-permute-start(f32[18,1,128]{2,1,0:T(1,128)S(1)} %get-tuple-element.37), channel_id=1, source_target_pairs={{0,1},{1,2},{2,3},{3,4},{4,5},{5,6},{6,7},{7,8},{8,9},{9,10},{10,1... | collective-permute-start | bytes 27656 | tf_op jit(solution)/shard_map/ppermute | solution.py:24
  391.1 34.2 %collective-permute-start.42 = (f32[1,16,128]{2,1,0:T(8,128)S(1)}, f32[1,16,128]{2,1,0:T(8,128)S(1)}, u32[]{:S(2)}, u32[]{:S(2)}) collective-permute-start(f32[1,16,128]{2,1,0:T(8,128)S(1)} %slice.583), channel_id=1, source_target_pairs={{0,16},{16,32},{32,48},{48,64},{64,80},{80,96},{96,112},{112,128},... | collective-permute-start | bytes 24584 | tf_op jit(solution)/shard_map/ppermute | solution.py:24
  398.3 15.5 %collective-permute-start.35 = (f32[1,16,128]{2,1,0:T(8,128)S(1)}, f32[1,16,128]{2,1,0:T(8,128)S(1)}, u32[]{:S(2)}, u32[]{:S(2)}) collective-permute-start(f32[1,16,128]{2,1,0:T(8,128)S(1)} %get-tuple-element.24), channel_id=1, source_target_pairs={{0,16},{16,32},{32,48},{48,64},{64,80},{80,96},{96,112},{112,128},... | collective-permute-start | bytes 24584 | tf_op jit(solution)/shard_map/ppermute | solution.py:24
  400.2 13.5 %collective-permute-start.36 = (f32[1,16,128]{2,1,0:T(8,128)S(1)}, f32[1,16,128]{2,1,0:T(8,128)S(1)}, u32[]{:S(2)}, u32[]{:S(2)}) collective-permute-start(f32[1,16,128]{2,1,0:T(8,128)S(1)} %get-tuple-element.25), channel_id=1, source_target_pairs={{16,0},{32,16},{48,32},{64,48},{80,64},{96,80},{112,96},{128,112},... | collective-permute-start | bytes 24584 | tf_op jit(solution)/shard_map/ppermute | solution.py:26
  406.1 9.7 %collective-permute-start.38 = (f32[1,16,128]{2,1,0:T(8,128)S(1)}, f32[1,16,128]{2,1,0:T(8,128)S(1)}, u32[]{:S(2)}, u32[]{:S(2)}) collective-permute-start(f32[1,16,128]{2,1,0:T(8,128)S(1)} %get-tuple-element.47), channel_id=1, source_target_pairs={{0,16},{16,32},{32,48},{48,64},{64,80},{80,96},{96,112},{112,128},... | collective-permute-start | bytes 24584 | tf_op jit(solution)/shard_map/ppermute | solution.py:24
  408.0 7.7 %collective-permute-start.39 = (f32[1,16,128]{2,1,0:T(8,128)S(1)}, f32[1,16,128]{2,1,0:T(8,128)S(1)}, u32[]{:S(2)}, u32[]{:S(2)}) collective-permute-start(f32[1,16,128]{2,1,0:T(8,128)S(1)} %get-tuple-element.46), channel_id=1, source_target_pairs={{16,0},{32,16},{48,32},{64,48},{80,64},{96,80},{112,96},{128,112},... | collective-permute-start | bytes 24584 | tf_op jit(solution)/shard_map/ppermute | solution.py:26
  413.8 13.5 %collective-permute-start.37 = (f32[18,1,128]{2,1,0:T(1,128)S(1)}, f32[18,1,128]{2,1,0:T(1,128)S(1)}, u32[]{:S(2)}, u32[]{:S(2)}) collective-permute-start(f32[18,1,128]{2,1,0:T(1,128)S(1)} %pad_maximum_fusion.63), channel_id=1, source_target_pairs={{0,1},{1,2},{2,3},{3,4},{4,5},{5,6},{6,7},{7,8},{8,9},{9,10},{10,1... | collective-permute-start | bytes 27656 | tf_op jit(solution)/shard_map/ppermute | solution.py:24
  415.8 11.6 %collective-permute-start.40 = (f32[18,1,128]{2,1,0:T(1,128)S(1)}, f32[18,1,128]{2,1,0:T(1,128)S(1)}, u32[]{:S(2)}, u32[]{:S(2)}) collective-permute-start(f32[18,1,128]{2,1,0:T(1,128)S(1)} %get-tuple-element.34), channel_id=1, source_target_pairs={{1,0},{2,1},{3,2},{4,3},{5,4},{6,5},{7,6},{8,7},{9,8},{10,9},{11,1... | collective-permute-start | bytes 27656 | tf_op jit(solution)/shard_map/ppermute | solution.py:26
  423.3 9.2 %collective-permute-start.41 = (f32[18,1,128]{2,1,0:T(1,128)S(1)}, f32[18,1,128]{2,1,0:T(1,128)S(1)}, u32[]{:S(2)}, u32[]{:S(2)}) collective-permute-start(f32[18,1,128]{2,1,0:T(1,128)S(1)} %get-tuple-element.35), channel_id=1, source_target_pairs={{0,1},{1,2},{2,3},{3,4},{4,5},{5,6},{6,7},{7,8},{8,9},{9,10},{10,1... | collective-permute-start | bytes 27656 | tf_op jit(solution)/shard_map/ppermute | solution.py:24
  425.4 34.2 %collective-permute-start.50 = (f32[1,16,128]{2,1,0:T(8,128)S(1)}, f32[1,16,128]{2,1,0:T(8,128)S(1)}, u32[]{:S(2)}, u32[]{:S(2)}) collective-permute-start(f32[1,16,128]{2,1,0:T(8,128)S(1)} %slice.594), channel_id=1, source_target_pairs={{0,16},{16,32},{32,48},{48,64},{64,80},{80,96},{96,112},{112,128},... | collective-permute-start | bytes 24584 | tf_op jit(solution)/shard_map/ppermute | solution.py:24
  432.6 15.5 %collective-permute-start.43 = (f32[1,16,128]{2,1,0:T(8,128)S(1)}, f32[1,16,128]{2,1,0:T(8,128)S(1)}, u32[]{:S(2)}, u32[]{:S(2)}) collective-permute-start(f32[1,16,128]{2,1,0:T(8,128)S(1)} %get-tuple-element.22), channel_id=1, source_target_pairs={{0,16},{16,32},{32,48},{48,64},{64,80},{80,96},{96,112},{112,128},... | collective-permute-start | bytes 24584 | tf_op jit(solution)/shard_map/ppermute | solution.py:24
  434.6 13.5 %collective-permute-start.44 = (f32[1,16,128]{2,1,0:T(8,128)S(1)}, f32[1,16,128]{2,1,0:T(8,128)S(1)}, u32[]{:S(2)}, u32[]{:S(2)}) collective-permute-start(f32[1,16,128]{2,1,0:T(8,128)S(1)} %get-tuple-element.23), channel_id=1, source_target_pairs={{16,0},{32,16},{48,32},{64,48},{80,64},{96,80},{112,96},{128,112},... | collective-permute-start | bytes 24584 | tf_op jit(solution)/shard_map/ppermute | solution.py:26
  440.4 9.7 %collective-permute-start.46 = (f32[1,16,128]{2,1,0:T(8,128)S(1)}, f32[1,16,128]{2,1,0:T(8,128)S(1)}, u32[]{:S(2)}, u32[]{:S(2)}) collective-permute-start(f32[1,16,128]{2,1,0:T(8,128)S(1)} %get-tuple-element.44), channel_id=1, source_target_pairs={{0,16},{16,32},{32,48},{48,64},{64,80},{80,96},{96,112},{112,128},... | collective-permute-start | bytes 24584 | tf_op jit(solution)/shard_map/ppermute | solution.py:24
  448.1 11.6 %collective-permute-start.45 = (f32[18,1,128]{2,1,0:T(1,128)S(1)}, f32[18,1,128]{2,1,0:T(1,128)S(1)}, u32[]{:S(2)}, u32[]{:S(2)}) collective-permute-start(f32[18,1,128]{2,1,0:T(1,128)S(1)} %pad_maximum_fusion.58), channel_id=1, source_target_pairs={{0,1},{1,2},{2,3},{3,4},{4,5},{5,6},{6,7},{7,8},{8,9},{9,10},{10,1... | collective-permute-start | bytes 27656 | tf_op jit(solution)/shard_map/ppermute | solution.py:24
  450.1 9.6 %collective-permute-start.48 = (f32[18,1,128]{2,1,0:T(1,128)S(1)}, f32[18,1,128]{2,1,0:T(1,128)S(1)}, u32[]{:S(2)}, u32[]{:S(2)}) collective-permute-start(f32[18,1,128]{2,1,0:T(1,128)S(1)} %get-tuple-element.32), channel_id=1, source_target_pairs={{1,0},{2,1},{3,2},{4,3},{5,4},{6,5},{7,6},{8,7},{9,8},{10,9},{11,1... | collective-permute-start | bytes 27656 | tf_op jit(solution)/shard_map/ppermute | solution.py:26
  457.7 9.2 %collective-permute-start.49 = (f32[18,1,128]{2,1,0:T(1,128)S(1)}, f32[18,1,128]{2,1,0:T(1,128)S(1)}, u32[]{:S(2)}, u32[]{:S(2)}) collective-permute-start(f32[18,1,128]{2,1,0:T(1,128)S(1)} %get-tuple-element.33), channel_id=1, source_target_pairs={{0,1},{1,2},{2,3},{3,4},{4,5},{5,6},{6,7},{7,8},{8,9},{9,10},{10,1... | collective-permute-start | bytes 27656 | tf_op jit(solution)/shard_map/ppermute | solution.py:24
  (19 other events, 220.1 us)
Sparse Core Ops, SparseCore 0:
  59.1 213.0 reduce-scatter.1
